TPU v7x, 32 devices: a whole 2x2x4 slice. The times are simulated.
32 devices in a mesh: comp: 8 (over z, y), seq: 4 (over x, core).
Axes of the slice: x: 2, y: 2, z: 4, core: 2. Of those that a mesh axis runs over, the one named last changes fastest.
Arguments:
- queries: bfloat16 [8, 512, 4096], P('comp', 'seq'), may hold values from -24 to 24
- keys: bfloat16 [8, 512, 4096], P('comp', 'seq'), may hold values from -24 to 24
- values: bfloat16 [8, 512, 4096], P('comp', 'seq'), may hold values from -6 to 6
- latent: float32 [64, 512], P('comp', 'seq'), may hold values from -6 to 6
- prev_denoised: float32 [64, 512], P('comp', 'seq'), may hold values from -6 to 6
- head_weight: bfloat16 [4096, 64], P('seq'), may hold values from -0.09375 to 0.09375
Outputs:
- hidden: bfloat16 [8, 512, 4096], P('comp', 'seq')
- new_latent: float32 [64, 512], P('comp', 'seq')
- denoised: float32 [64, 512], P('comp', 'seq')
All inputs are finite; a program needn't handle non-finite values.
Results may differ from a plain program's by a relative error of at most 0.008.
Values may be sent and summed in bfloat16 or wider, within the bound.
A program may use at most 64 MiB of HBM per device.

v0:
```python
import math

import jax
import jax.numpy as jnp
from jax import lax
from jax.sharding import PartitionSpec as P

HD = 128


alpha_now = 0.6
sigma_now = 0.8
alpha_next = 0.8
sigma_next = 0.6
step_before = 0.4


def broadcast(block, axis, source):
    block = jnp.where(lax.axis_index(axis) == source, block, jnp.zeros_like(block))
    return lax.psum(block, axis)


def group_attention(query_grp, key_grp, value_grp):
    length = query_grp.shape[0]
    block = math.gcd(length, 512)
    scale = query_grp.shape[2] ** (-0.5)

    def one_block(query_block):
        scores = (
            jnp.einsum("qgd,kgd->gqk", query_block, key_grp, preferred_element_type=jnp.float32)
            * scale
        )
        highest = jnp.max(scores, axis=2, keepdims=True)
        weights = jnp.exp(scores - highest)
        totals = jnp.sum(weights, axis=2, keepdims=True)
        probs = (weights / totals).astype(jnp.bfloat16)
        return jnp.einsum(
            "gqk,kgd->qgd", probs, value_grp, preferred_element_type=jnp.float32
        ).astype(jnp.bfloat16)

    blocks = query_grp.reshape(length // block, block, query_grp.shape[1], query_grp.shape[2])
    return lax.map(one_block, blocks).reshape(query_grp.shape)


def on_device(queries, keys, values, latent, prev_denoised, head_weight):
    seq_count = lax.axis_size("seq")
    local_tokens = queries.shape[1]
    width = queries.shape[2]
    per_device = width // HD // seq_count
    grouped_shape = (local_tokens, seq_count, per_device, HD)
    query_tok = queries[0].reshape(grouped_shape)
    key_tok = keys[0].reshape(grouped_shape)
    value_tok = values[0].reshape(grouped_shape)
    query_heads, key_heads, value_heads = (
        lax.all_to_all(query_tok, "seq", split_axis=1, concat_axis=0, tiled=True),
        lax.all_to_all(key_tok, "seq", split_axis=1, concat_axis=0, tiled=True),
        lax.all_to_all(value_tok, "seq", split_axis=1, concat_axis=0, tiled=True),
    )
    head_layout = group_attention(query_heads[:, 0], key_heads[:, 0], value_heads[:, 0])[:, None]
    returned = lax.all_to_all(head_layout, "seq", split_axis=0, concat_axis=1, tiled=True)
    hidden_tok = returned.reshape(local_tokens, width)
    squares = jnp.sum(jnp.square(hidden_tok.astype(jnp.float32)), axis=1)
    projected = jnp.dot(
        hidden_tok,
        lax.all_gather(head_weight, "seq", axis=0, tiled=True),
        preferred_element_type=jnp.float32,
    )
    norm_root = jnp.sqrt(squares / width + 1e-06)
    noise_all = (projected / norm_root[:, None]).T
    comp_count = lax.axis_size("comp")
    own_channels = latent.shape[0]
    position = lax.axis_index("comp")
    everyone = broadcast(noise_all.astype(jnp.bfloat16), "comp", comp_count - 1).astype(
        noise_all.dtype
    )
    noise_own = lax.dynamic_slice_in_dim(everyone, position * own_channels, own_channels, 0)
    denoised = (latent - sigma_now * noise_own) / alpha_now
    step_now = math.log(alpha_next / sigma_next) - math.log(alpha_now / sigma_now)
    ratio = step_before / step_now
    blend = (1.0 + 0.5 / ratio) * denoised - 0.5 / ratio * prev_denoised
    new_latent = sigma_next / sigma_now * latent - alpha_next * (math.exp(-step_now) - 1.0) * blend
    return (hidden_tok[None], new_latent, denoised)


def solution(mesh):
    return jax.shard_map(
        on_device,
        mesh=mesh,
        in_specs=(
            P("comp", "seq", None),
            P("comp", "seq", None),
            P("comp", "seq", None),
            P("comp", "seq"),
            P("comp", "seq"),
            P("seq", None),
        ),
        out_specs=(P("comp", "seq", None), P("comp", "seq"), P("comp", "seq")),
        check_vma=False,
    )
```

profile of v0, /device:TPU:0, one launch (start us, length us, event | category | flops | bytes accessed | tf_op | source)
XLA Modules:
  0.0 135.8 jit_solution(4760874608913296651)
XLA Ops:
  0.6 1.6 %copy.38 = bf16[1,128,4096]{1,2,0:T(8,128)(2,1)S(1)} copy(bf16[1,128,4096]{2,1,0:T(8,128)(2,1)} %param.6) | data formatting | bytes 2097152 | tf_op args[0]
  2.3 1.3 copy.39
  3.6 4.2 %all-to-all-start = ((bf16[128,4,8,128]{3,0,2,1:T(8,128)(2,1)}), bf16[128,4,8,128]{3,0,2,1:T(8,128)(2,1)S(1)}, u32[]{:S(2)}, u32[]{:S(2)}) async-start(bf16[128,4,8,128]{3,0,2,1:T(8,128)(2,1)} %copy.39), calls=%async_computation | async-start | bytes 2097152 | tf_op jit(solution)/shard_map/all_to_all | solution.py:55
  7.8 1.6 %copy.41 = bf16[1,128,4096]{1,2,0:T(8,128)(2,1)S(1)} copy(bf16[1,128,4096]{2,1,0:T(8,128)(2,1)} %param.7) | data formatting | bytes 2097152 | tf_op args[1]
  9.4 1.3 copy.42
  10.7 11.5 %all-to-all-done = bf16[128,4,8,128]{3,0,2,1:T(8,128)(2,1)S(1)} async-done(((bf16[128,4,8,128]{3,0,2,1:T(8,128)(2,1)}), bf16[128,4,8,128]{3,0,2,1:T(8,128)(2,1)S(1)}, u32[]{:S(2)}, u32[]{:S(2)}) %all-to-all-start) | async-done | bytes 1048608 | tf_op jit(solution)/shard_map/all_to_all | solution.py:55
  22.2 3.5 %all-to-all-start.1 = ((bf16[128,4,8,128]{3,0,2,1:T(8,128)(2,1)}), bf16[128,4,8,128]{3,0,2,1:T(8,128)(2,1)S(1)}, u32[]{:S(2)}, u32[]{:S(2)}) async-start(bf16[128,4,8,128]{3,0,2,1:T(8,128)(2,1)} %copy.42), calls=%async_computation.1 | async-start | bytes 2097152 | tf_op jit(solution)/shard_map/all_to_all | solution.py:56
  25.8 1.6 %copy.44 = bf16[1,128,4096]{1,2,0:T(8,128)(2,1)S(1)} copy(bf16[1,128,4096]{2,1,0:T(8,128)(2,1)} %param.8) | data formatting | bytes 2097152 | tf_op args[2]
  27.4 1.3 copy.45
  28.7 11.5 %all-to-all-done.1 = bf16[128,4,8,128]{3,0,2,1:T(8,128)(2,1)S(1)} async-done(((bf16[128,4,8,128]{3,0,2,1:T(8,128)(2,1)}), bf16[128,4,8,128]{3,0,2,1:T(8,128)(2,1)S(1)}, u32[]{:S(2)}, u32[]{:S(2)}) %all-to-all-start.1) | async-done | bytes 1048608 | tf_op jit(solution)/shard_map/all_to_all | solution.py:56
  40.2 3.5 %all-to-all-start.2 = ((bf16[128,4,8,128]{3,0,2,1:T(8,128)(2,1)}), bf16[128,4,8,128]{3,0,2,1:T(8,128)(2,1)S(1)}, u32[]{:S(2)}, u32[]{:S(2)}) async-start(bf16[128,4,8,128]{3,0,2,1:T(8,128)(2,1)} %copy.45), calls=%async_computation.2 | async-start | bytes 2097152 | tf_op jit(solution)/shard_map/all_to_all | solution.py:57
  43.7 1.1 copy.40
  44.8 0.1 copy.43
  44.9 13.2 %all-to-all-done.2 = bf16[128,4,8,128]{3,0,2,1:T(8,128)(2,1)S(1)} async-done(((bf16[128,4,8,128]{3,0,2,1:T(8,128)(2,1)}), bf16[128,4,8,128]{3,0,2,1:T(8,128)(2,1)S(1)}, u32[]{:S(2)}, u32[]{:S(2)}) %all-to-all-start.2) | async-done | bytes 1048608 | tf_op jit(solution)/shard_map/all_to_all | solution.py:57
  58.1 0.1 copy.46
  58.3 7.1 %fusion.15 = (f32[8,512]{1,0:T(8,128)S(1)}, f32[8,512,512]{1,2,0:T(8,128)}) fusion(bf16[512,8,128]{2,0,1:T(8,128)(2,1)} %bitcast.43, bf16[512,8,128]{2,0,1:T(8,128)(2,1)S(1)} %bitcast.44), kind=kOutput, calls=%fused_computation.20 | convolution fusion | flops 543162880 | bytes 10502144 | tf_op jit(solution)/shard_map/while/body/eval_jaxpr/sub | solution.py:34
  65.4 4.9 %fusion.7 = bf16[512,1,8,128]{3,0,2,1:T(8,128)(2,1)S(1)} fusion(bf16[512,8,128]{2,0,1:T(8,128)(2,1)S(1)} %bitcast.45, f32[8,512,512]{1,2,0:T(8,128)} %get-tuple-element.30, f32[8,512]{1,0:T(8,128)S(1)} %get-tuple-element.29), kind=kOutput, calls=%fused_computation.9 | convolution fusion | flops 541589504 | bytes 10502144 | tf_op jit(solution)/shard_map/while/body/eval_jaxpr/gqk,kgd->qgd/dot_general | solution.py:37
  70.3 0.0 copy-start.1
  70.3 0.0 copy-start.2
  70.3 1.6 %copy.48 = bf16[512,1,8,128]{3,2,1,0:T(8,128)(2,1)} copy(bf16[512,1,8,128]{3,0,2,1:T(8,128)(2,1)S(1)} %fusion.7) | data formatting | bytes 2097152 | tf_op jit(solution)/shard_map/broadcast_in_dim;reshape | solution.py:59
  71.9 3.5 %all-to-all-start.3 = ((bf16[512,1,8,128]{3,2,1,0:T(8,128)(2,1)}), bf16[512,1,8,128]{3,2,1,0:T(8,128)(2,1)S(1)}, u32[]{:S(2)}, u32[]{:S(2)}) async-start(bf16[512,1,8,128]{3,2,1,0:T(8,128)(2,1)} %copy.48), calls=%async_computation.3 | async-start | bytes 2097152 | tf_op jit(solution)/shard_map/all_to_all | solution.py:60
  75.5 0.0 copy-done
  75.5 18.1 %all_gather.3 = bf16[4096,64]{0,1:T(8,128)(2,1)S(1)} all-gather(bf16[1024,64]{0,1:T(8,128)(2,1)S(1)} %copy-done), channel_id=1, replica_groups=mesh['comp'=8,'seq'=4] {'seq'}, dimensions={0}, use_global_device_ids=true | all-gather | bytes 655360 | tf_op jit(solution)/shard_map/all_gather | solution.py:65
  93.6 0.0 all-to-all-done.3
  93.6 0.8 copy.49
  94.3 1.0 multiply_reduce_fusion.1
  95.4 0.3 fusion.10
  95.7 38.1 %psum.7 = bf16[64,128]{1,0:T(8,128)(2,1)S(1)} all-reduce(bf16[64,128]{1,0:T(8,128)(2,1)S(1)} %fusion.10), channel_id=1, replica_groups=mesh['comp'=8,'seq'=4] {'comp'}, use_global_device_ids=true, to_apply=%region_3.4 | all-reduce | flops 8192 | bytes 32768 | tf_op jit(solution)/shard_map/psum | solution.py:20
  133.9 1.3 copy.51
  135.2 0.0 copy-done.1
  135.2 0.0 copy-done.2
  135.2 0.6 fusion.13
  (2 shorter events, 0.0 us)
Async XLA Ops:
  3.6 18.7 %all-to-all-start = ((bf16[128,4,8,128]{3,0,2,1:T(8,128)(2,1)}), bf16[128,4,8,128]{3,0,2,1:T(8,128)(2,1)S(1)}, u32[]{:S(2)}, u32[]{:S(2)}) async-start(bf16[128,4,8,128]{3,0,2,1:T(8,128)(2,1)} %copy.39), calls=%async_computation | async-start | bytes 2097152 | tf_op jit(solution)/shard_map/all_to_all | solution.py:55
  22.2 18.0 %all-to-all-start.1 = ((bf16[128,4,8,128]{3,0,2,1:T(8,128)(2,1)}), bf16[128,4,8,128]{3,0,2,1:T(8,128)(2,1)S(1)}, u32[]{:S(2)}, u32[]{:S(2)}) async-start(bf16[128,4,8,128]{3,0,2,1:T(8,128)(2,1)} %copy.42), calls=%async_computation.1 | async-start | bytes 2097152 | tf_op jit(solution)/shard_map/all_to_all | solution.py:56
  40.2 18.0 %all-to-all-start.2 = ((bf16[128,4,8,128]{3,0,2,1:T(8,128)(2,1)}), bf16[128,4,8,128]{3,0,2,1:T(8,128)(2,1)S(1)}, u32[]{:S(2)}, u32[]{:S(2)}) async-start(bf16[128,4,8,128]{3,0,2,1:T(8,128)(2,1)} %copy.45), calls=%async_computation.2 | async-start | bytes 2097152 | tf_op jit(solution)/shard_map/all_to_all | solution.py:57
  65.4 10.1 %copy-start = (bf16[1024,64]{0,1:T(8,128)(2,1)S(1)}, bf16[1024,64]{0,1:T(8,128)(2,1)}, u32[]{:S(2)}) copy-start(bf16[1024,64]{0,1:T(8,128)(2,1)} %param.11) | copy-start | bytes 393220
  70.3 64.9 %copy-start.1 = (f32[8,128]{1,0:T(8,128)S(1)}, f32[8,128]{1,0:T(8,128)}, u32[]{:S(2)}) copy-start(f32[8,128]{1,0:T(8,128)} %param.9) | copy-start | bytes 12292
  70.3 64.9 %copy-start.2 = (f32[8,128]{1,0:T(8,128)S(1)}, f32[8,128]{1,0:T(8,128)}, u32[]{:S(2)}) copy-start(f32[8,128]{1,0:T(8,128)} %param.10) | copy-start | bytes 12292
  71.9 21.6 %all-to-all-start.3 = ((bf16[512,1,8,128]{3,2,1,0:T(8,128)(2,1)}), bf16[512,1,8,128]{3,2,1,0:T(8,128)(2,1)S(1)}, u32[]{:S(2)}, u32[]{:S(2)}) async-start(bf16[512,1,8,128]{3,2,1,0:T(8,128)(2,1)} %copy.48), calls=%async_computation.3 | async-start | bytes 2097152 | tf_op jit(solution)/shard_map/all_to_all | solution.py:60
where the time goes:
time: 136 us
  blocking collectives  56.2 us (41%)
  waiting for transfers between devices  36.2 us (27%)
  starting transfers between devices  14.8 us (11%)
  local copies, waits for them, and re-layouts  13.9 us (10%)
  matrix products  12.3 us (9%)
  other arithmetic  1.65 us (1%)
    psum x1, blocking collectives, broadcast(): return lax.psum(block, axis)  38.1 us
    all_gather x1, blocking collectives, on_device(): lax.all_gather(head_weight, 'seq', axis=0, tiled=True)  18.1 us
    all_to_all x1, waiting for transfers between devices, on_device(): lax.all_to_all(value_tok, 'seq', split_axis=1, concat_axis=0, tiled=True)  13.2 us
    all_to_all x1, waiting for transfers between devices, on_device(): lax.all_to_all(query_tok, 'seq', split_axis=1, concat_axis=0, tiled=True)  11.5 us
    all_to_all x1, waiting for transfers between devices, on_device(): lax.all_to_all(key_tok, 'seq', split_axis=1, concat_axis=0, tiled=True)  11.5 us
    sub x1, matrix products, one_block(): weights = jnp.exp(scores - highest)  7.13 us
    unnamed x10, local copies, waits for them, and re-layouts  6.16 us
    dot_general x1, matrix products, one_block(): jnp.einsum('gqk,kgd->qgd', probs, value_grp, preferred_element_type=jnp.f...  4.86 us
  transfers between devices with their start and end apart: 4, of which 3 were waited for; matrix products, arithmetic and copies ran while one was open for 5% of the time, Pallas kernels for 0%

commit v1 on v0

v1 whole, which is shorter than its diff:
```python
import functools
import math

import jax
import jax.numpy as jnp
from jax import lax
from jax.experimental import pallas as pl
from jax.experimental.pallas import tpu as pltpu
from jax.sharding import PartitionSpec as P

HD = 128
CHUNKS = 8
MESH = pl.DeviceIdType.MESH

alpha_now = 0.6
sigma_now = 0.8
alpha_next = 0.8
sigma_next = 0.6
step_before = 0.4


def kernel(
    n, comps, own, q_hbm, k_hbm, v_hbm, w_hbm, hid_hbm, noise_ref,
    kbuf, vbuf, qbuf, obuf, wbuf, acc, sq, nsend, nrecv,
    k_send, k_recv, v_send, v_recv, q_send, q_recv, q_local,
    o_send, o_recv, o_local, w_send, w_recv, n_send, n_recv,
):
    tokens, width = hid_hbm.shape
    half = width // 2
    chips = n // 2
    cw = half // CHUNKS
    rows_w = width // n
    pad = nsend.shape[2] - 8
    comp = lax.axis_index("comp")
    me = lax.axis_index("seq")
    chip, core = me // 2, me % 2
    mate = chip * 2 + 1 - core
    last = comp == comps - 1

    def peer(d_chip, d_core):
        return lax.rem(chip + d_chip, chips) * 2 + lax.rem(core + d_core, 2)

    barrier = pltpu.get_barrier_semaphore()
    others = [(dx, dc) for dx in range(chips) for dc in range(2) if (dx, dc) != (0, 0)]
    for dx, dc in others:
        pl.semaphore_signal(barrier, inc=1, device_id=(comp, peer(dx, dc)), device_id_type=MESH)

    @pl.when(jnp.logical_not(last))
    def _():
        for target in (me, mate):
            pl.semaphore_signal(
                barrier, inc=1, device_id=(comps - 1, target), device_id_type=MESH
            )
        pl.semaphore_wait(barrier, n - 1)

    @pl.when(last)
    def _():
        pl.semaphore_wait(barrier, n - 1 + 2 * (comps - 1))

    def columns(side, j):
        return pl.ds(pl.multiple_of(side * half + j * cw, cw), cw)

    def kept(j):
        return pl.ds(pl.multiple_of(j * cw, cw), cw)

    def remote(src, dst, send, recv, target):
        return pltpu.make_async_remote_copy(
            src_ref=src, dst_ref=dst, send_sem=send, recv_sem=recv,
            device_id=(comp, target), device_id_type=MESH,
        )

    def kv_copies(dx, dc, j):
        target = peer(dx, dc)
        side = lax.rem(core + dc, 2)
        slot = ((chips - dx) % chips) * 2 + dc
        return [
            remote(src.at[0, :, columns(side, j)], buf.at[slot, :, kept(j)],
                   send.at[slot, j], recv.at[slot, j], target)
            for src, buf, send, recv in (
                (k_hbm, kbuf, k_send, k_recv), (v_hbm, vbuf, v_send, v_recv))
        ]

    def q_copy(j):
        return remote(q_hbm.at[0, :, columns(1 - core, j)], qbuf.at[1, :, kept(j)],
                      q_send.at[j], q_recv.at[j], mate)

    def local_copies(j):
        mine = columns(core, j)
        return [
            pltpu.make_async_copy(q_hbm.at[0, :, mine], qbuf.at[0, :, kept(j)], q_local.at[j]),
            pltpu.make_async_copy(k_hbm.at[0, :, mine], kbuf.at[0, :, kept(j)], k_recv.at[0, j]),
            pltpu.make_async_copy(v_hbm.at[0, :, mine], vbuf.at[0, :, kept(j)], v_recv.at[0, j]),
        ]

    def o_copies(j):
        mine = columns(core, j)
        return [
            pltpu.make_async_copy(obuf.at[0, :, kept(j)], hid_hbm.at[:, mine], o_local.at[j]),
            remote(obuf.at[1, :, kept(j)], hid_hbm.at[:, mine], o_send.at[j], o_recv.at[j], mate),
        ]

    w_side = me // chips
    w_slot = lax.rem(me, chips)

    def w_copy(x):
        return remote(w_hbm, wbuf.at[w_slot], w_send.at[x], w_recv.at[w_slot], x * 2 + w_side)

    @pl.when(last)
    def _():
        for x in range(chips):
            @pl.when(x * 2 + w_side != me)
            def _():
                w_copy(x).start()

            @pl.when(x * 2 + w_side == me)
            def _():
                pltpu.make_async_copy(w_hbm, wbuf.at[w_slot], w_recv.at[w_slot]).start()

        acc[...] = jnp.zeros_like(acc)
        sq[...] = jnp.zeros_like(sq)

    def start_chunk(j, carry):
        for dx in range(1, chips):
            for dc in range(2):
                for copy in kv_copies(dx, dc, j):
                    copy.start()
        for copy in kv_copies(0, 1, j):
            copy.start()
        q_copy(j).start()
        for copy in local_copies(j):
            copy.start()
        return carry

    lax.fori_loop(0, CHUNKS, start_chunk, 0)

    @pl.when(last)
    def _():
        for x in range(chips):
            pltpu.make_async_copy(w_hbm, wbuf.at[x], w_recv.at[x]).wait()

    factor = HD ** (-0.5) * math.log2(math.e)

    def attend(j, carry):
        for copy in local_copies(j):
            copy.wait()
        q_copy(j).wait_recv()
        for dx, dc in others:
            for copy in kv_copies(dx, dc, j):
                copy.wait_recv()
        for h in range(cw // HD):
            cols = pl.ds(pl.multiple_of(j * cw + h * HD, HD), HD)
            query = qbuf[:, :, cols].reshape(2 * tokens, HD)
            key = kbuf[:, :, cols].reshape(n * tokens, HD)
            value = vbuf[:, :, cols].reshape(n * tokens, HD)
            scores = lax.dot_general(
                query, key, (((1,), (1,)), ((), ())), preferred_element_type=jnp.float32
            )
            highest = jnp.max(scores, axis=1, keepdims=True)
            weights = jnp.exp2((scores - highest) * factor)
            totals = jnp.sum(weights, axis=1, keepdims=True)
            out = jnp.dot(weights.astype(jnp.bfloat16), value, preferred_element_type=jnp.float32)
            out = (out / totals).astype(jnp.bfloat16)
            obuf[:, :, cols] = out.reshape(2, tokens, HD)
        for copy in o_copies(j):
            copy.start()

        @pl.when(last)
        def _():
            part = obuf[:, :, kept(j)].reshape(2 * tokens, cw)
            rows = wbuf.reshape(half, wbuf.shape[2])[kept(j), :]
            acc[...] += jnp.dot(part, rows, preferred_element_type=jnp.float32)
            wide = part.astype(jnp.float32)
            sq[...] += jnp.sum(wide * wide, axis=1, keepdims=True)

        return carry

    lax.fori_loop(0, CHUNKS, attend, 0)

    def noise_copy(c, side):
        return pltpu.make_async_remote_copy(
            src_ref=nsend.at[c, side], dst_ref=nrecv.at[side],
            send_sem=n_send.at[c, side], recv_sem=n_recv.at[side],
            device_id=(c, me if side == 0 else mate), device_id_type=MESH,
        )

    def noise_self():
        return pltpu.make_async_copy(nsend.at[comps - 1, 0], nrecv.at[0], n_recv.at[0])

    @pl.when(last)
    def _():
        both = jnp.concatenate([acc[...], jnp.broadcast_to(sq[...], acc.shape)], axis=1).T
        channels = acc.shape[1]
        for c in range(comps):
            for side in range(2):
                toks = slice(side * tokens, (side + 1) * tokens)
                nsend[c, side, 0:own, :] = both[c * own:(c + 1) * own, toks]
                nsend[c, side, pad:pad + 8, :] = both[channels:channels + 8, toks]
        for c in range(comps):
            for side in range(2):
                if (c, side) == (comps - 1, 0):
                    noise_self().start()
                else:
                    noise_copy(c, side).start()

    def drain(j, carry):
        for dx, dc in others:
            for copy in kv_copies(dx, dc, j):
                copy.wait_send()
        q_copy(j).wait_send()
        local, back = o_copies(j)
        local.wait()
        back.wait()
        return carry

    lax.fori_loop(0, CHUNKS, drain, 0)

    @pl.when(last)
    def _():
        for x in range(chips):
            @pl.when(x * 2 + w_side != me)
            def _():
                w_copy(x).wait_send()
        for c in range(comps):
            for side in range(2):
                if (c, side) != (comps - 1, 0):
                    noise_copy(c, side).wait_send()

    for side in range(2):
        pltpu.make_async_copy(nsend.at[0, side], nrecv.at[side], n_recv.at[side]).wait()
    total = nrecv[0] + nrecv[1]
    root = jnp.sqrt(total[pad:pad + 1] / width + 1e-06)
    noise_ref[...] = total[0:own] / root


def on_device(queries, keys, values, latent, prev_denoised, head_weight):
    n = lax.axis_size("seq")
    comps = lax.axis_size("comp")
    _, tokens, width = queries.shape
    half = width // 2
    own = latent.shape[0]
    channels = head_weight.shape[1]
    pad = -(-own // 8) * 8
    bf16, f32 = jnp.bfloat16, jnp.float32
    dma = pltpu.SemaphoreType.DMA
    anywhere = pl.BlockSpec(memory_space=pl.ANY)
    hidden, noise_own = pl.pallas_call(
        functools.partial(kernel, n, comps, own),
        out_shape=(
            jax.ShapeDtypeStruct((tokens, width), bf16),
            jax.ShapeDtypeStruct((own, tokens), f32),
        ),
        in_specs=[anywhere] * 4,
        out_specs=(anywhere, pl.BlockSpec(memory_space=pltpu.VMEM)),
        scratch_shapes=[
            pltpu.VMEM((n, tokens, half), bf16),
            pltpu.VMEM((n, tokens, half), bf16),
            pltpu.VMEM((2, tokens, half), bf16),
            pltpu.VMEM((2, tokens, half), bf16),
            pltpu.VMEM((n // 2, width // n, channels), bf16),
            pltpu.VMEM((2 * tokens, channels), f32),
            pltpu.VMEM((2 * tokens, 1), f32),
            pltpu.VMEM((comps, 2, pad + 8, tokens), f32),
            pltpu.VMEM((2, pad + 8, tokens), f32),
            dma((n, CHUNKS)), dma((n, CHUNKS)), dma((n, CHUNKS)), dma((n, CHUNKS)),
            dma((CHUNKS,)), dma((CHUNKS,)), dma((CHUNKS,)),
            dma((CHUNKS,)), dma((CHUNKS,)), dma((CHUNKS,)),
            dma((n // 2,)), dma((n // 2,)),
            dma((comps, 2)), dma((2,)),
        ],
        compiler_params=pltpu.CompilerParams(
            collective_id=0, has_side_effects=True, vmem_limit_bytes=48 * 1024 * 1024
        ),
        name="attention_step",
    )(queries, keys, values, head_weight)
    denoised = (latent - sigma_now * noise_own) / alpha_now
    step_now = math.log(alpha_next / sigma_next) - math.log(alpha_now / sigma_now)
    ratio = step_before / step_now
    blend = (1.0 + 0.5 / ratio) * denoised - 0.5 / ratio * prev_denoised
    new_latent = sigma_next / sigma_now * latent - alpha_next * (math.exp(-step_now) - 1.0) * blend
    return (hidden[None], new_latent, denoised)


def solution(mesh):
    return jax.shard_map(
        on_device,
        mesh=mesh,
        in_specs=(
            P("comp", "seq", None),
            P("comp", "seq", None),
            P("comp", "seq", None),
            P("comp", "seq"),
            P("comp", "seq"),
            P("seq", None),
        ),
        out_specs=(P("comp", "seq", None), P("comp", "seq"), P("comp", "seq")),
        check_vma=False,
    )
```

time: 136 us -> 71.6 us (0.53)
  Pallas kernels: 0 us -> 63.7 us
  blocking collectives: 56.2 us -> 0 us
  waiting for transfers between devices: 36.2 us -> 0 us
  starting transfers between devices: 14.8 us -> 0 us
  matrix products: 12.3 us -> 0 us
  local copies, waits for them, and re-layouts: 13.9 us -> 6.39 us
    pallas_call x0 -> x1, Pallas kernels: none -> 63.7 us  [on_device(): pl.pallas_call(functools.partial(kernel, n, comps, own), out_shape=(jax.S...]
    psum x1 -> x0, blocking collectives: 38.1 us -> none  [broadcast(): return lax.psum(block, axis)]
    all_to_all x4 -> x0, waiting for transfers between devices: 36.2 us -> none  [the longest x1 13.2 us: on_device(): lax.all_to_all(value_tok, 'seq', split_axis=1, concat_axis=0, tiled=True)]
    all_gather x1 -> x0, blocking collectives: 18.1 us -> none  [on_device(): lax.all_gather(head_weight, 'seq', axis=0, tiled=True)]
    all_to_all x4 -> x0, starting transfers between devices: 14.8 us -> none  [the longest x1 4.21 us: on_device(): lax.all_to_all(query_tok, 'seq', split_axis=1, concat_axis=0, tiled=True)]
    sub x1 -> x0, matrix products: 7.13 us -> none  [one_block(): weights = jnp.exp(scores - highest)]
    another operation x4 -> x0, local copies, waits for them, and re-layouts: 5.58 us -> none  [the longest x1 1.65 us: on_device(): group_attention(query_heads[:, 0], key_heads[:, 0], value_heads[:, 0])]
    dot_general x2 -> x0, matrix products: 5.18 us -> none  [the longest x1 4.86 us: one_block(): jnp.einsum('gqk,kgd->qgd', probs, value_grp, preferred_element_type=jnp.f...]
  transfers between devices with their start and end apart: 4 -> 0, of which waited for: 3 -> 0; matrix products, arithmetic and copies ran while one was open for 5% -> 0% of each run, Pallas kernels for 0% -> 0%
where the time goes in v1:
time: 71.6 us; the launch traced here: 71.3 us
  Pallas kernels  63.7 us (89%)
  local copies, waits for them, and re-layouts  6.39 us (9%)
    pallas_call x1, Pallas kernels, on_device(): pl.pallas_call(functools.partial(kernel, n, comps, own), out_shape=(jax.S...  63.7 us
    unnamed x12, local copies, waits for them, and re-layouts  6.39 us

profile of v1, /device:TPU:0, one launch (start us, length us, event | category | flops | bytes accessed | tf_op | source)
XLA Modules:
  0.0 71.3 jit_solution(2873585330791168542)
XLA Ops:
  0.6 1.1 %copy.9.w_hbm = bf16[1024,64]{1,0:T(8,128)(2,1)S(1)} copy(bf16[1024,64]{0,1:T(8,128)(2,1)} %param.11) | data formatting | bytes 262144 | tf_op args[5]
  1.7 0.0 copy-start
  1.7 1.2 %copy-done = bf16[1,128,4096]{2,1,0:T(8,128)(2,1)S(1)} copy-done((bf16[1,128,4096]{2,1,0:T(8,128)(2,1)S(1)}, bf16[1,128,4096]{2,1,0:T(8,128)(2,1)}, u32[]{:S(2)}) %copy-start) | copy-done | bytes 1048600
  2.9 0.0 copy-start.1
  2.9 1.2 %copy-done.1 = bf16[1,128,4096]{2,1,0:T(8,128)(2,1)S(1)} copy-done((bf16[1,128,4096]{2,1,0:T(8,128)(2,1)S(1)}, bf16[1,128,4096]{2,1,0:T(8,128)(2,1)}, u32[]{:S(2)}) %copy-start.1) | copy-done | bytes 1048600
  4.2 0.0 copy-start.2
  4.2 1.2 %copy-done.2 = bf16[1,128,4096]{2,1,0:T(8,128)(2,1)S(1)} copy-done((bf16[1,128,4096]{2,1,0:T(8,128)(2,1)S(1)}, bf16[1,128,4096]{2,1,0:T(8,128)(2,1)}, u32[]{:S(2)}) %copy-start.2) | copy-done | bytes 1048600
  5.4 0.0 copy-start.4
  5.4 63.7 %attention_step.1 = (bf16[128,4096]{1,0:T(8,128)(2,1)S(1)}, f32[8,128]{1,0:T(8,128)S(1)}) custom-call(bf16[1,128,4096]{2,1,0:T(8,128)(2,1)S(1)} %copy-done, bf16[1,128,4096]{2,1,0:T(8,128)(2,1)S(1)} %copy-done.1, bf16[1,128,4096]{2,1,0:T(8,128)(2,1)S(1)} %copy-done.2, bf16[1024,64]{1,0:T(8,128)(2,1)S(1)} %copy.9.w_hbm), custom_call_target="tpu_custom_call" | custom-call | tf_op jit(solution)/shard_map/attention_step/pallas_call | solution.py:246
  69.1 0.0 copy-start.3
  69.1 0.0 copy-done.4
  69.1 0.7 copy-done.3
  69.8 0.6 broadcast_multiply_fusion
  70.4 1.0 %copy.11 = bf16[1,128,4096]{2,1,0:T(8,128)(2,1)} copy(bf16[1,128,4096]{2,1,0:T(8,128)(2,1)S(1)} %bitcast.1) | data formatting | bytes 2097152
Async XLA Ops:
  1.7 1.2 %copy-start = (bf16[1,128,4096]{2,1,0:T(8,128)(2,1)S(1)}, bf16[1,128,4096]{2,1,0:T(8,128)(2,1)}, u32[]{:S(2)}) copy-start(bf16[1,128,4096]{2,1,0:T(8,128)(2,1)} %q_hbm.1) | copy-start | bytes 3145732
  2.9 1.2 %copy-start.1 = (bf16[1,128,4096]{2,1,0:T(8,128)(2,1)S(1)}, bf16[1,128,4096]{2,1,0:T(8,128)(2,1)}, u32[]{:S(2)}) copy-start(bf16[1,128,4096]{2,1,0:T(8,128)(2,1)} %k_hbm.1) | copy-start | bytes 3145732
  4.2 1.2 %copy-start.2 = (bf16[1,128,4096]{2,1,0:T(8,128)(2,1)S(1)}, bf16[1,128,4096]{2,1,0:T(8,128)(2,1)}, u32[]{:S(2)}) copy-start(bf16[1,128,4096]{2,1,0:T(8,128)(2,1)} %v_hbm.1) | copy-start | bytes 3145732
  5.4 63.7 %copy-start.4 = (f32[8,128]{1,0:T(8,128)S(1)}, f32[8,128]{1,0:T(8,128)}, u32[]{:S(2)}) copy-start(f32[8,128]{1,0:T(8,128)} %param.10) | copy-start | bytes 12292
  69.1 0.7 copy-start.3

commit v2 on v1

--- a/solution.py
+++ b/solution.py
@@ -10,6 +10,7 @@
 
 HD = 128
 CHUNKS = 8
+WINDOW = 3
 MESH = pl.DeviceIdType.MESH
 
 alpha_now = 0.6
@@ -131,7 +132,7 @@
             copy.start()
         return carry
 
-    lax.fori_loop(0, CHUNKS, start_chunk, 0)
+    lax.fori_loop(0, WINDOW, start_chunk, 0)
 
     @pl.when(last)
     def _():
@@ -147,6 +148,11 @@
         for dx, dc in others:
             for copy in kv_copies(dx, dc, j):
                 copy.wait_recv()
+
+        @pl.when(j + WINDOW < CHUNKS)
+        def _():
+            start_chunk(j + WINDOW, 0)
+
         for h in range(cw // HD):
             cols = pl.ds(pl.multiple_of(j * cw + h * HD, HD), HD)
             query = qbuf[:, :, cols].reshape(2 * tokens, HD)
@@ -167,8 +173,11 @@
         @pl.when(last)
         def _():
             part = obuf[:, :, kept(j)].reshape(2 * tokens, cw)
-            rows = wbuf.reshape(half, wbuf.shape[2])[kept(j), :]
-            acc[...] += jnp.dot(part, rows, preferred_element_type=jnp.float32)
+            first = j * cw
+            rows = wbuf[first // rows_w, :, pl.ds(pl.multiple_of(first % rows_w, cw), cw)]
+            acc[...] += lax.dot_general(
+                part, rows, (((1,), (1,)), ((), ())), preferred_element_type=jnp.float32
+            )
             wide = part.astype(jnp.float32)
             sq[...] += jnp.sum(wide * wide, axis=1, keepdims=True)
 
@@ -256,7 +265,7 @@
             pltpu.VMEM((n, tokens, half), bf16),
             pltpu.VMEM((2, tokens, half), bf16),
             pltpu.VMEM((2, tokens, half), bf16),
-            pltpu.VMEM((n // 2, width // n, channels), bf16),
+            pltpu.VMEM((n // 2, channels, width // n), bf16),
             pltpu.VMEM((2 * tokens, channels), f32),
             pltpu.VMEM((2 * tokens, 1), f32),
             pltpu.VMEM((comps, 2, pad + 8, tokens), f32),
@@ -268,10 +277,10 @@
             dma((comps, 2)), dma((2,)),
         ],
         compiler_params=pltpu.CompilerParams(
-            collective_id=0, has_side_effects=True, vmem_limit_bytes=48 * 1024 * 1024
+            collective_id=0, has_side_effects=True, vmem_limit_bytes=60 * 1024 * 1024
         ),
         name="attention_step",
-    )(queries, keys, values, head_weight)
+    )(queries, keys, values, head_weight.T)
     denoised = (latent - sigma_now * noise_own) / alpha_now
     step_now = math.log(alpha_next / sigma_next) - math.log(alpha_now / sigma_now)
     ratio = step_before / step_now

time: 71.6 us -> 66.8 us (0.933)
  local copies, waits for them, and re-layouts: 6.39 us -> 2.96 us
  Pallas kernels: 63.7 us -> 61.7 us
    unnamed x12 -> x5, local copies, waits for them, and re-layouts: 6.39 us -> 2.96 us
    pallas_call x1, Pallas kernels: 63.7 us -> 61.7 us  [on_device(): pl.pallas_call(functools.partial(kernel, n, comps, own), out_shape=(jax.S...]
where the time goes in v2:
time: 66.8 us; the launch traced here: 66.6 us
  Pallas kernels  61.7 us (92%)
  local copies, waits for them, and re-layouts  2.96 us (4%)
  other arithmetic  1.27 us (2%)
    pallas_call x1, Pallas kernels, on_device(): pl.pallas_call(functools.partial(kernel, n, comps, own), out_shape=(jax.S...  61.7 us
    unnamed x5, local copies, waits for them, and re-layouts  2.96 us

profile of v2, /device:TPU:0, one launch (start us, length us, event | category | flops | bytes accessed | tf_op | source)
XLA Modules:
  0.0 66.6 jit_solution(1669559465098469586)
XLA Ops:
  0.6 0.0 copy-start.1
  0.6 61.7 %attention_step.1 = (bf16[128,4096]{1,0:T(8,128)(2,1)}, f32[8,128]{1,0:T(8,128)}) custom-call(bf16[1,128,4096]{2,1,0:T(8,128)(2,1)} %q_hbm.1, bf16[1,128,4096]{2,1,0:T(8,128)(2,1)} %k_hbm.1, bf16[1,128,4096]{2,1,0:T(8,128)(2,1)} %v_hbm.1, bf16[64,1024]{1,0:T(8,128)(2,1)} %bitcast.3), custom_call_target="tpu_custom_call" | custom-call | tf_op jit(solution)/shard_map/attention_step/pallas_call | solution.py:255
  62.3 0.0 copy-start
  62.3 0.0 copy-done.1
  62.3 0.7 %copy-done = f32[8,128]{1,0:T(8,128)S(1)} copy-done((f32[8,128]{1,0:T(8,128)S(1)}, f32[8,128]{1,0:T(8,128)}, u32[]{:S(2)}) %copy-start) | copy-done | bytes 4120
  63.0 1.3 %broadcast_multiply_fusion = (f32[8,128]{1,0:T(8,128)}, f32[8,128]{1,0:T(8,128)}) fusion(f32[8,128]{1,0:T(8,128)S(1)} %copy-done, f32[8,128]{1,0:T(8,128)} %get-tuple-element.6, f32[8,128]{1,0:T(8,128)S(1)} %copy-done.1), kind=kLoop, calls=%fused_computation.2 | loop fusion | flops 9216 | bytes 20480 | tf_op jit(solution)/shard_map/div | solution.py:284
  64.3 2.3 %copy.10 = bf16[1,128,4096]{2,1,0:T(8,128)(2,1)} copy(bf16[1,128,4096]{2,1,0:T(8,128)(2,1)} %bitcast.2) | data formatting | bytes 2097152
Async XLA Ops:
  0.6 61.7 %copy-start.1 = (f32[8,128]{1,0:T(8,128)S(1)}, f32[8,128]{1,0:T(8,128)}, u32[]{:S(2)}) copy-start(f32[8,128]{1,0:T(8,128)} %param.10) | copy-start | bytes 12292
  62.3 0.7 %copy-start = (f32[8,128]{1,0:T(8,128)S(1)}, f32[8,128]{1,0:T(8,128)}, u32[]{:S(2)}) copy-start(f32[8,128]{1,0:T(8,128)} %param.9) | copy-start | bytes 12292

commit v3 on v2

--- a/solution.py
+++ b/solution.py
@@ -11,6 +11,7 @@
 HD = 128
 CHUNKS = 8
 WINDOW = 3
+LATE = 5
 MESH = pl.DeviceIdType.MESH
 
 alpha_now = 0.6
@@ -22,9 +23,11 @@
 
 def kernel(
     n, comps, own, q_hbm, k_hbm, v_hbm, w_hbm, hid_hbm, noise_ref,
-    kbuf, vbuf, qbuf, obuf, wbuf, acc, sq, nsend, nrecv,
+    kbuf, vbuf, qbuf, obuf, wbuf, acc, sq, nsend, nrecv, relay_in, relay_mid, w_mid,
     k_send, k_recv, v_send, v_recv, q_send, q_recv, q_local,
     o_send, o_recv, o_local, w_send, w_recv, n_send, n_recv,
+    in_send, in_recv, mid_send, mid_recv, back_send, piece_recv,
+    wm_send, wm_recv, wb_send, w_piece, ready,
 ):
     tokens, width = hid_hbm.shape
     half = width // 2
@@ -46,17 +49,26 @@
     for dx, dc in others:
         pl.semaphore_signal(barrier, inc=1, device_id=(comp, peer(dx, dc)), device_id_type=MESH)
 
+    @pl.when(last)
+    def _():
+        for c in range(comps - 1):
+            for target in (me, mate):
+                pl.semaphore_signal(barrier, inc=1, device_id=(c, target), device_id_type=MESH)
+        pl.semaphore_wait(barrier, n - 1)
+
     @pl.when(jnp.logical_not(last))
     def _():
+        pl.semaphore_wait(barrier, n + 1)
         for target in (me, mate):
-            pl.semaphore_signal(
-                barrier, inc=1, device_id=(comps - 1, target), device_id_type=MESH
-            )
-        pl.semaphore_wait(barrier, n - 1)
-
-    @pl.when(last)
-    def _():
-        pl.semaphore_wait(barrier, n - 1 + 2 * (comps - 1))
+            pl.semaphore_signal(ready, inc=1, device_id=(comps - 1, target), device_id_type=MESH)
+
+    pieces, piece_rows = piece_recv.shape[0], relay_in.shape[2]
+    w_pieces, piece_cols = w_piece.shape[0], w_mid.shape[2]
+    helper = jnp.logical_and(jnp.logical_not(last), comp >= comps - pieces)
+    w_helper = jnp.logical_and(jnp.logical_not(last), comp >= comps - w_pieces)
+    final = CHUNKS - 1
+    far = [(dx, dc) for dx in range(1, chips) for dc in range(2)]
+    far_slots = [((chips - dx) % chips) * 2 + dc for dx, dc in far]
 
     def columns(side, j):
         return pl.ds(pl.multiple_of(side * half + j * cw, cw), cw)
@@ -64,10 +76,10 @@
     def kept(j):
         return pl.ds(pl.multiple_of(j * cw, cw), cw)
 
-    def remote(src, dst, send, recv, target):
+    def remote(src, dst, send, recv, target, owner=comp):
         return pltpu.make_async_remote_copy(
             src_ref=src, dst_ref=dst, send_sem=send, recv_sem=recv,
-            device_id=(comp, target), device_id_type=MESH,
+            device_id=(owner, target), device_id_type=MESH,
         )
 
     def kv_copies(dx, dc, j):
@@ -100,31 +112,118 @@
             remote(obuf.at[1, :, kept(j)], hid_hbm.at[:, mine], o_send.at[j], o_recv.at[j], mate),
         ]
 
+    def piece(i):
+        return pl.ds(i * piece_rows, piece_rows)
+
+    def direct_copies(dx, dc):
+        slot = ((chips - dx) % chips) * 2 + dc
+        side = lax.rem(core + dc, 2)
+        return [
+            remote(src.at[0, piece(pieces - 1), columns(side, final)],
+                   buf.at[slot, piece(pieces - 1), kept(final)],
+                   send.at[slot, final], piece_recv.at[pieces - 1, slot, kind], peer(dx, dc))
+            for kind, (src, buf, send) in enumerate(
+                ((k_hbm, kbuf, k_send), (v_hbm, vbuf, v_send)))
+        ]
+
+    def out_copies(i):
+        return [
+            remote(src.at[0, piece(i), columns(side, final)], relay_in.at[kind, side],
+                   in_send.at[i, kind, side], in_recv.at[kind, side],
+                   me, comps - pieces + i)
+            for kind, src in enumerate((k_hbm, v_hbm)) for side in range(2)
+        ]
+
+    def across_copies():
+        copies = []
+        for (dx, dc), slot in zip(far, far_slots):
+            for kind in range(2):
+                copies.append(remote(
+                    relay_in.at[kind, lax.rem(core + dc, 2)], relay_mid.at[slot, kind],
+                    mid_send.at[slot, kind], mid_recv.at[slot, kind], peer(dx, dc)))
+        return copies
+
+    def back_copies(i):
+        return [
+            remote(relay_mid.at[slot, kind], buf.at[slot, piece(i), kept(final)],
+                   back_send.at[slot, kind], piece_recv.at[i, slot, kind], me, comps - 1)
+            for slot in far_slots for kind, buf in enumerate((kbuf, vbuf))
+        ]
+
+    def piece_arrivals(i):
+        return [
+            pltpu.make_async_copy(buf.at[slot, piece(i), kept(final)],
+                                  buf.at[slot, piece(i), kept(final)],
+                                  piece_recv.at[i, slot, kind])
+            for slot in far_slots for kind, buf in enumerate((kbuf, vbuf))
+        ]
+
     w_side = me // chips
     w_slot = lax.rem(me, chips)
 
-    def w_copy(x):
-        return remote(w_hbm, wbuf.at[w_slot], w_send.at[x], w_recv.at[w_slot], x * 2 + w_side)
+    def w_cols(i):
+        return pl.ds(i * piece_cols, piece_cols)
+
+    def w_near():
+        return remote(w_hbm, wbuf.at[w_slot], w_send.at[chips], w_recv.at[w_slot],
+                      chip * 2 + w_side)
+
+    def w_direct(x):
+        return remote(w_hbm.at[:, w_cols(w_pieces - 1)], wbuf.at[w_slot, :, w_cols(w_pieces - 1)],
+                      w_send.at[x], w_piece.at[w_pieces - 1, w_slot], x * 2 + w_side)
+
+    def w_across(i, x):
+        return remote(w_hbm.at[:, w_cols(i)], w_mid.at[w_slot],
+                      wm_send.at[x], wm_recv.at[w_slot], x * 2 + w_side)
+
+    def w_back(i, x):
+        return remote(w_mid.at[x], wbuf.at[x, :, w_cols(i)],
+                      wb_send.at[x], w_piece.at[i, x], me, comps - 1)
+
+    def is_near(slot):
+        return (core * chips + slot) // 2 == chip
 
     @pl.when(last)
     def _():
+        @pl.when(chip * 2 + w_side != me)
+        def _():
+            w_near().start()
+
+        @pl.when(chip * 2 + w_side == me)
+        def _():
+            pltpu.make_async_copy(w_hbm, wbuf.at[w_slot], w_recv.at[w_slot]).start()
+
         for x in range(chips):
-            @pl.when(x * 2 + w_side != me)
-            def _():
-                w_copy(x).start()
-
-            @pl.when(x * 2 + w_side == me)
-            def _():
-                pltpu.make_async_copy(w_hbm, wbuf.at[w_slot], w_recv.at[w_slot]).start()
+            @pl.when(x != chip)
+            def _():
+                w_direct(x).start()
 
         acc[...] = jnp.zeros_like(acc)
         sq[...] = jnp.zeros_like(sq)
 
+    for i in range(w_pieces - 1):
+        @pl.when(comp == comps - w_pieces + i)
+        def _():
+            for x in range(chips):
+                @pl.when(x != chip)
+                def _():
+                    w_across(i, x).start()
+
     def start_chunk(j, carry):
-        for dx in range(1, chips):
-            for dc in range(2):
+        cut = jnp.logical_and(last, j == final)
+
+        @pl.when(jnp.logical_not(cut))
+        def _():
+            for dx, dc in far:
                 for copy in kv_copies(dx, dc, j):
                     copy.start()
+
+        @pl.when(cut)
+        def _():
+            for dx, dc in far:
+                for copy in direct_copies(dx, dc):
+                    copy.start()
+
         for copy in kv_copies(0, 1, j):
             copy.start()
         q_copy(j).start()
@@ -136,8 +235,60 @@
 
     @pl.when(last)
     def _():
+        pl.semaphore_wait(ready, 2 * (comps - 1))
+        for i in range(pieces - 1):
+            for copy in out_copies(i):
+                copy.start()
+
+    def relay_across():
+        @pl.when(helper)
+        def _():
+            for copy in out_copies(0):
+                copy.wait_recv()
+            for copy in across_copies():
+                copy.start()
+
+    def relay_back():
+        @pl.when(helper)
+        def _():
+            for copy in across_copies():
+                copy.wait_recv()
+        for i in range(pieces - 1):
+            @pl.when(comp == comps - pieces + i)
+            def _():
+                for copy in back_copies(i):
+                    copy.start()
+        for i in range(w_pieces - 1):
+            @pl.when(comp == comps - w_pieces + i)
+            def _():
+                for x in range(chips):
+                    @pl.when(jnp.logical_not(is_near(x)))
+                    def _():
+                        pltpu.make_async_copy(w_mid.at[x], w_mid.at[x], wm_recv.at[x]).wait()
+                        w_back(i, x).start()
+
+    def await_rows():
         for x in range(chips):
-            pltpu.make_async_copy(w_hbm, wbuf.at[x], w_recv.at[x]).wait()
+            @pl.when(is_near(x))
+            def _():
+                pltpu.make_async_copy(wbuf.at[x], wbuf.at[x], w_recv.at[x]).wait()
+
+            @pl.when(jnp.logical_not(is_near(x)))
+            def _():
+                for i in range(w_pieces):
+                    dst = wbuf.at[x, :, w_cols(i)]
+                    pltpu.make_async_copy(dst, dst, w_piece.at[i, x]).wait()
+
+    def project(j, carry):
+        part = obuf[:, :, kept(j)].reshape(2 * tokens, cw)
+        first = j * cw
+        rows = wbuf[first // rows_w, :, pl.ds(pl.multiple_of(first % rows_w, cw), cw)]
+        acc[...] += lax.dot_general(
+            part, rows, (((1,), (1,)), ((), ())), preferred_element_type=jnp.float32
+        )
+        wide = part.astype(jnp.float32)
+        sq[...] += jnp.sum(wide * wide, axis=1, keepdims=True)
+        return carry
 
     factor = HD ** (-0.5) * math.log2(math.e)
 
@@ -145,9 +296,24 @@
         for copy in local_copies(j):
             copy.wait()
         q_copy(j).wait_recv()
-        for dx, dc in others:
-            for copy in kv_copies(dx, dc, j):
-                copy.wait_recv()
+        for copy in kv_copies(0, 1, j):
+            copy.wait_recv()
+        cut = jnp.logical_and(last, j == final)
+
+        @pl.when(jnp.logical_not(cut))
+        def _():
+            for dx, dc in far:
+                for copy in kv_copies(dx, dc, j):
+                    copy.wait_recv()
+
+        @pl.when(cut)
+        def _():
+            for i in range(pieces):
+                for copy in piece_arrivals(i):
+                    copy.wait()
+
+        pl.when(j == 1)(relay_across)
+        pl.when(j == 3)(relay_back)
 
         @pl.when(j + WINDOW < CHUNKS)
         def _():
@@ -170,16 +336,14 @@
         for copy in o_copies(j):
             copy.start()
 
-        @pl.when(last)
-        def _():
-            part = obuf[:, :, kept(j)].reshape(2 * tokens, cw)
-            first = j * cw
-            rows = wbuf[first // rows_w, :, pl.ds(pl.multiple_of(first % rows_w, cw), cw)]
-            acc[...] += lax.dot_general(
-                part, rows, (((1,), (1,)), ((), ())), preferred_element_type=jnp.float32
-            )
-            wide = part.astype(jnp.float32)
-            sq[...] += jnp.sum(wide * wide, axis=1, keepdims=True)
+        @pl.when(jnp.logical_and(last, j == LATE))
+        def _():
+            await_rows()
+            lax.fori_loop(0, LATE + 1, project, 0)
+
+        @pl.when(jnp.logical_and(last, j > LATE))
+        def _():
+            project(j, 0)
 
         return carry
 
@@ -212,9 +376,22 @@
                     noise_copy(c, side).start()
 
     def drain(j, carry):
-        for dx, dc in others:
-            for copy in kv_copies(dx, dc, j):
-                copy.wait_send()
+        cut = jnp.logical_and(last, j == final)
+
+        @pl.when(jnp.logical_not(cut))
+        def _():
+            for dx, dc in far:
+                for copy in kv_copies(dx, dc, j):
+                    copy.wait_send()
+
+        @pl.when(cut)
+        def _():
+            for dx, dc in far:
+                for copy in direct_copies(dx, dc):
+                    copy.wait_send()
+
+        for copy in kv_copies(0, 1, j):
+            copy.wait_send()
         q_copy(j).wait_send()
         local, back = o_copies(j)
         local.wait()
@@ -223,12 +400,35 @@
 
     lax.fori_loop(0, CHUNKS, drain, 0)
 
+    @pl.when(helper)
+    def _():
+        for copy in across_copies() + back_copies(0):
+            copy.wait_send()
+
+    @pl.when(w_helper)
+    def _():
+        for x in range(chips):
+            @pl.when(x != chip)
+            def _():
+                w_across(0, x).wait_send()
+
+            @pl.when(jnp.logical_not(is_near(x)))
+            def _():
+                w_back(0, x).wait_send()
+
     @pl.when(last)
     def _():
+        @pl.when(chip * 2 + w_side != me)
+        def _():
+            w_near().wait_send()
+
         for x in range(chips):
-            @pl.when(x * 2 + w_side != me)
-            def _():
-                w_copy(x).wait_send()
+            @pl.when(x != chip)
+            def _():
+                w_direct(x).wait_send()
+        for i in range(pieces - 1):
+            for copy in out_copies(i):
+                copy.wait_send()
         for c in range(comps):
             for side in range(2):
                 if (c, side) != (comps - 1, 0):
@@ -249,14 +449,17 @@
     own = latent.shape[0]
     channels = head_weight.shape[1]
     pad = -(-own // 8) * 8
+    chips, rows_w = n // 2, width // n
+    pieces = min(comps, tokens // 16)
+    w_pieces = min(comps, rows_w // 128)
     bf16, f32 = jnp.bfloat16, jnp.float32
     dma = pltpu.SemaphoreType.DMA
     anywhere = pl.BlockSpec(memory_space=pl.ANY)
     hidden, noise_own = pl.pallas_call(
         functools.partial(kernel, n, comps, own),
         out_shape=(
-            jax.ShapeDtypeStruct((tokens, width), bf16),
-            jax.ShapeDtypeStruct((own, tokens), f32),
+            pltpu.VMEM((tokens, width), bf16),
+            pltpu.VMEM((own, tokens), f32),
         ),
         in_specs=[anywhere] * 4,
         out_specs=(anywhere, pl.BlockSpec(memory_space=pltpu.VMEM)),
@@ -270,11 +473,18 @@
             pltpu.VMEM((2 * tokens, 1), f32),
             pltpu.VMEM((comps, 2, pad + 8, tokens), f32),
             pltpu.VMEM((2, pad + 8, tokens), f32),
+            pltpu.VMEM((2, 2, tokens // pieces, half // CHUNKS), bf16),
+            pltpu.VMEM((n, 2, tokens // pieces, half // CHUNKS), bf16),
+            pltpu.VMEM((chips, channels, rows_w // w_pieces), bf16),
             dma((n, CHUNKS)), dma((n, CHUNKS)), dma((n, CHUNKS)), dma((n, CHUNKS)),
             dma((CHUNKS,)), dma((CHUNKS,)), dma((CHUNKS,)),
             dma((CHUNKS,)), dma((CHUNKS,)), dma((CHUNKS,)),
-            dma((n // 2,)), dma((n // 2,)),
+            dma((chips + 1,)), dma((chips,)),
             dma((comps, 2)), dma((2,)),
+            dma((pieces, 2, 2)), dma((2, 2)), dma((n, 2)), dma((n, 2)), dma((n, 2)),
+            dma((pieces, n, 2)),
+            dma((chips,)), dma((chips,)), dma((chips,)), dma((w_pieces, chips)),
+            pltpu.SemaphoreType.REGULAR,
         ],
         compiler_params=pltpu.CompilerParams(
             collective_id=0, has_side_effects=True, vmem_limit_bytes=60 * 1024 * 1024

time: 66.8 us -> 61.7 us (0.924)
  Pallas kernels: 61.7 us -> 59.3 us
  local copies, waits for them, and re-layouts: 2.96 us -> 0.99 us
  other arithmetic: 1.27 us -> 0.6 us
    pallas_call x1, Pallas kernels: 61.7 us -> 59.3 us  [on_device(): pl.pallas_call(functools.partial(kernel, n, comps, own), out_shape=(pltpu...]
    unnamed x5, local copies, waits for them, and re-layouts: 2.96 us -> 0.99 us
    div x1, other arithmetic: 1.27 us -> 0.6 us  [on_device(): denoised = (latent - sigma_now * noise_own) / alpha_now]
where the time goes in v3:
time: 61.7 us; the launch traced here: 61.5 us
  Pallas kernels  59.3 us (96%)
  local copies, waits for them, and re-layouts  0.99 us (2%)
  between operations  0.66 us (1%)
    pallas_call x1, Pallas kernels, on_device(): pl.pallas_call(functools.partial(kernel, n, comps, own), out_shape=(pltpu...  59.3 us

profile of v3, /device:TPU:0, one launch (start us, length us, event | category | flops | bytes accessed | tf_op | source)
XLA Modules:
  0.0 61.5 jit_solution(1937863927640900741)
XLA Ops:
  0.6 59.3 %attention_step.1 = (bf16[128,4096]{1,0:T(8,128)(2,1)S(1)}, f32[8,128]{1,0:T(8,128)S(1)}) custom-call(bf16[1,128,4096]{2,1,0:T(8,128)(2,1)} %q_hbm.1, bf16[1,128,4096]{2,1,0:T(8,128)(2,1)} %k_hbm.1, bf16[1,128,4096]{2,1,0:T(8,128)(2,1)} %v_hbm.1, bf16[64,1024]{1,0:T(8,128)(2,1)} %bitcast.3), custom_call_target="tpu_custom_call" | custom-call | tf_op jit(solution)/shard_map/attention_step/pallas_call | solution.py:458
  59.9 0.0 copy-start
  59.9 0.0 copy-start.1
  60.0 1.0 %copy.10 = bf16[1,128,4096]{2,1,0:T(8,128)(2,1)} copy(bf16[1,128,4096]{2,1,0:T(8,128)(2,1)S(1)} %bitcast.2) | data formatting | bytes 2097152
  60.9 0.0 copy-done
  60.9 0.0 copy-done.1
  60.9 0.6 broadcast_multiply_fusion
Async XLA Ops:
  59.9 1.0 %copy-start = (f32[8,128]{1,0:T(8,128)S(1)}, f32[8,128]{1,0:T(8,128)}, u32[]{:S(2)}) copy-start(f32[8,128]{1,0:T(8,128)} %param.9) | copy-start | bytes 12292
  59.9 1.0 %copy-start.1 = (f32[8,128]{1,0:T(8,128)S(1)}, f32[8,128]{1,0:T(8,128)}, u32[]{:S(2)}) copy-start(f32[8,128]{1,0:T(8,128)} %param.10) | copy-start | bytes 12292

commit v4 on v3

--- a/solution.py
+++ b/solution.py
@@ -10,7 +10,7 @@
 
 HD = 128
 CHUNKS = 8
-WINDOW = 3
+WINDOW = 2
 LATE = 5
 MESH = pl.DeviceIdType.MESH
 
@@ -27,7 +27,7 @@
     k_send, k_recv, v_send, v_recv, q_send, q_recv, q_local,
     o_send, o_recv, o_local, w_send, w_recv, n_send, n_recv,
     in_send, in_recv, mid_send, mid_recv, back_send, piece_recv,
-    wm_send, wm_recv, wb_send, w_piece, ready,
+    wm_send, wm_recv, wb_send, w_piece,
 ):
     tokens, width = hid_hbm.shape
     half = width // 2
@@ -49,18 +49,17 @@
     for dx, dc in others:
         pl.semaphore_signal(barrier, inc=1, device_id=(comp, peer(dx, dc)), device_id_type=MESH)
 
+    @pl.when(jnp.logical_not(last))
+    def _():
+        for target in (me, mate):
+            pl.semaphore_signal(
+                barrier, inc=1, device_id=(comps - 1, target), device_id_type=MESH
+            )
+        pl.semaphore_wait(barrier, n - 1)
+
     @pl.when(last)
     def _():
-        for c in range(comps - 1):
-            for target in (me, mate):
-                pl.semaphore_signal(barrier, inc=1, device_id=(c, target), device_id_type=MESH)
-        pl.semaphore_wait(barrier, n - 1)
-
-    @pl.when(jnp.logical_not(last))
-    def _():
-        pl.semaphore_wait(barrier, n + 1)
-        for target in (me, mate):
-            pl.semaphore_signal(ready, inc=1, device_id=(comps - 1, target), device_id_type=MESH)
+        pl.semaphore_wait(barrier, n - 1 + 2 * (comps - 1))
 
     pieces, piece_rows = piece_recv.shape[0], relay_in.shape[2]
     w_pieces, piece_cols = w_piece.shape[0], w_mid.shape[2]
@@ -235,7 +234,6 @@
 
     @pl.when(last)
     def _():
-        pl.semaphore_wait(ready, 2 * (comps - 1))
         for i in range(pieces - 1):
             for copy in out_copies(i):
                 copy.start()
@@ -484,7 +482,6 @@
             dma((pieces, 2, 2)), dma((2, 2)), dma((n, 2)), dma((n, 2)), dma((n, 2)),
             dma((pieces, n, 2)),
             dma((chips,)), dma((chips,)), dma((chips,)), dma((w_pieces, chips)),
-            pltpu.SemaphoreType.REGULAR,
         ],
         compiler_params=pltpu.CompilerParams(
             collective_id=0, has_side_effects=True, vmem_limit_bytes=60 * 1024 * 1024

time: 61.7 us -> 58.3 us (0.945)
  Pallas kernels: 59.3 us -> 55.9 us
    pallas_call x1, Pallas kernels: 59.3 us -> 55.9 us  [on_device(): pl.pallas_call(functools.partial(kernel, n, comps, own), out_shape=(pltpu...]
where the time goes in v4:
time: 58.3 us; the launch traced here: 58.1 us
  Pallas kernels  55.9 us (96%)
  local copies, waits for them, and re-layouts  0.99 us (2%)
  between operations  0.66 us (1%)
  other arithmetic  0.6 us (1%)
    pallas_call x1, Pallas kernels, on_device(): pl.pallas_call(functools.partial(kernel, n, comps, own), out_shape=(pltpu...  55.9 us

profile of v4, /device:TPU:0, one launch (start us, length us, event | category | flops | bytes accessed | tf_op | source)
XLA Modules:
  0.0 58.1 jit_solution(10722504311612766450)
XLA Ops:
  0.6 55.9 %attention_step.1 = (bf16[128,4096]{1,0:T(8,128)(2,1)S(1)}, f32[8,128]{1,0:T(8,128)S(1)}) custom-call(bf16[1,128,4096]{2,1,0:T(8,128)(2,1)} %q_hbm.1, bf16[1,128,4096]{2,1,0:T(8,128)(2,1)} %k_hbm.1, bf16[1,128,4096]{2,1,0:T(8,128)(2,1)} %v_hbm.1, bf16[64,1024]{1,0:T(8,128)(2,1)} %bitcast.3), custom_call_target="tpu_custom_call" | custom-call | tf_op jit(solution)/shard_map/attention_step/pallas_call | solution.py:456
  56.5 0.0 copy-start
  56.5 0.0 copy-start.1
  56.5 1.0 %copy.10 = bf16[1,128,4096]{2,1,0:T(8,128)(2,1)} copy(bf16[1,128,4096]{2,1,0:T(8,128)(2,1)S(1)} %bitcast.2) | data formatting | bytes 2097152
  57.5 0.0 copy-done
  57.5 0.0 copy-done.1
  57.5 0.6 %broadcast_multiply_fusion = (f32[8,128]{1,0:T(8,128)}, f32[8,128]{1,0:T(8,128)}) fusion(f32[8,128]{1,0:T(8,128)S(1)} %copy-done, f32[8,128]{1,0:T(8,128)S(1)} %get-tuple-element.6, f32[8,128]{1,0:T(8,128)S(1)} %copy-done.1), kind=kLoop, calls=%fused_computation.2 | loop fusion | flops 9216 | bytes 20480 | tf_op jit(solution)/shard_map/div | solution.py:491
Async XLA Ops:
  56.5 1.0 %copy-start = (f32[8,128]{1,0:T(8,128)S(1)}, f32[8,128]{1,0:T(8,128)}, u32[]{:S(2)}) copy-start(f32[8,128]{1,0:T(8,128)} %param.9) | copy-start | bytes 12292
  56.5 1.0 %copy-start.1 = (f32[8,128]{1,0:T(8,128)S(1)}, f32[8,128]{1,0:T(8,128)}, u32[]{:S(2)}) copy-start(f32[8,128]{1,0:T(8,128)} %param.10) | copy-start | bytes 12292

commit v5 on v4

--- a/solution.py
+++ b/solution.py
@@ -9,9 +9,12 @@
 from jax.sharding import PartitionSpec as P
 
 HD = 128
-CHUNKS = 8
-WINDOW = 2
-LATE = 5
+SIZES = (4, 4, 4, 2, 1, 1)
+CHUNKS = len(SIZES)
+FIRST = tuple(sum(SIZES[:j]) for j in range(CHUNKS))
+FINAL = 3
+LATE = 3
+STARTS = {0: (2,), 1: (3,), 2: (4, 5)}
 MESH = pl.DeviceIdType.MESH
 
 alpha_now = 0.6
@@ -32,7 +35,7 @@
     tokens, width = hid_hbm.shape
     half = width // 2
     chips = n // 2
-    cw = half // CHUNKS
+    assert sum(SIZES) * HD == half
     rows_w = width // n
     pad = nsend.shape[2] - 8
     comp = lax.axis_index("comp")
@@ -65,15 +68,16 @@
     w_pieces, piece_cols = w_piece.shape[0], w_mid.shape[2]
     helper = jnp.logical_and(jnp.logical_not(last), comp >= comps - pieces)
     w_helper = jnp.logical_and(jnp.logical_not(last), comp >= comps - w_pieces)
-    final = CHUNKS - 1
+    final = FINAL
     far = [(dx, dc) for dx in range(1, chips) for dc in range(2)]
     far_slots = [((chips - dx) % chips) * 2 + dc for dx, dc in far]
 
     def columns(side, j):
-        return pl.ds(pl.multiple_of(side * half + j * cw, cw), cw)
+        start = pl.multiple_of(side * half + FIRST[j] * HD, HD)
+        return pl.ds(start, SIZES[j] * HD)
 
     def kept(j):
-        return pl.ds(pl.multiple_of(j * cw, cw), cw)
+        return pl.ds(FIRST[j] * HD, SIZES[j] * HD)
 
     def remote(src, dst, send, recv, target, owner=comp):
         return pltpu.make_async_remote_copy(
@@ -208,29 +212,32 @@
                 def _():
                     w_across(i, x).start()
 
-    def start_chunk(j, carry):
-        cut = jnp.logical_and(last, j == final)
-
-        @pl.when(jnp.logical_not(cut))
-        def _():
-            for dx, dc in far:
-                for copy in kv_copies(dx, dc, j):
-                    copy.start()
-
-        @pl.when(cut)
-        def _():
-            for dx, dc in far:
-                for copy in direct_copies(dx, dc):
-                    copy.start()
-
+    def start_far(j):
+        for dx, dc in far:
+            for copy in kv_copies(dx, dc, j):
+                copy.start()
+
+    def start_chunk(j):
+        if j == final:
+            @pl.when(jnp.logical_not(last))
+            def _():
+                start_far(j)
+
+            @pl.when(last)
+            def _():
+                for dx, dc in far:
+                    for copy in direct_copies(dx, dc):
+                        copy.start()
+        else:
+            start_far(j)
         for copy in kv_copies(0, 1, j):
             copy.start()
         q_copy(j).start()
         for copy in local_copies(j):
             copy.start()
-        return carry
-
-    lax.fori_loop(0, WINDOW, start_chunk, 0)
+
+    start_chunk(0)
+    start_chunk(1)
 
     @pl.when(last)
     def _():
@@ -277,75 +284,87 @@
                     dst = wbuf.at[x, :, w_cols(i)]
                     pltpu.make_async_copy(dst, dst, w_piece.at[i, x]).wait()
 
-    def project(j, carry):
-        part = obuf[:, :, kept(j)].reshape(2 * tokens, cw)
-        first = j * cw
-        rows = wbuf[first // rows_w, :, pl.ds(pl.multiple_of(first % rows_w, cw), cw)]
-        acc[...] += lax.dot_general(
-            part, rows, (((1,), (1,)), ((), ())), preferred_element_type=jnp.float32
-        )
-        wide = part.astype(jnp.float32)
-        sq[...] += jnp.sum(wide * wide, axis=1, keepdims=True)
-        return carry
+    def project(j):
+        unit = min(SIZES[j], 2) * HD
+        for first in range(FIRST[j] * HD, (FIRST[j] + SIZES[j]) * HD, unit):
+            part = obuf[:, :, first:first + unit].reshape(2 * tokens, unit)
+            at = first % rows_w
+            rows = wbuf[first // rows_w, :, at:at + unit]
+            acc[...] += lax.dot_general(
+                part, rows, (((1,), (1,)), ((), ())), preferred_element_type=jnp.float32
+            )
+            wide = part.astype(jnp.float32)
+            sq[...] += jnp.sum(wide * wide, axis=1, keepdims=True)
 
     factor = HD ** (-0.5) * math.log2(math.e)
 
-    def attend(j, carry):
+    def wait_far(j):
+        for dx, dc in far:
+            for copy in kv_copies(dx, dc, j):
+                copy.wait_recv()
+
+    def attend(j):
         for copy in local_copies(j):
             copy.wait()
         q_copy(j).wait_recv()
         for copy in kv_copies(0, 1, j):
             copy.wait_recv()
-        cut = jnp.logical_and(last, j == final)
-
-        @pl.when(jnp.logical_not(cut))
-        def _():
-            for dx, dc in far:
-                for copy in kv_copies(dx, dc, j):
-                    copy.wait_recv()
-
-        @pl.when(cut)
-        def _():
-            for i in range(pieces):
-                for copy in piece_arrivals(i):
-                    copy.wait()
-
-        pl.when(j == 1)(relay_across)
-        pl.when(j == 3)(relay_back)
-
-        @pl.when(j + WINDOW < CHUNKS)
-        def _():
-            start_chunk(j + WINDOW, 0)
-
-        for h in range(cw // HD):
-            cols = pl.ds(pl.multiple_of(j * cw + h * HD, HD), HD)
-            query = qbuf[:, :, cols].reshape(2 * tokens, HD)
-            key = kbuf[:, :, cols].reshape(n * tokens, HD)
-            value = vbuf[:, :, cols].reshape(n * tokens, HD)
-            scores = lax.dot_general(
-                query, key, (((1,), (1,)), ((), ())), preferred_element_type=jnp.float32
-            )
-            highest = jnp.max(scores, axis=1, keepdims=True)
-            weights = jnp.exp2((scores - highest) * factor)
-            totals = jnp.sum(weights, axis=1, keepdims=True)
-            out = jnp.dot(weights.astype(jnp.bfloat16), value, preferred_element_type=jnp.float32)
-            out = (out / totals).astype(jnp.bfloat16)
-            obuf[:, :, cols] = out.reshape(2, tokens, HD)
+        if j == final:
+            @pl.when(jnp.logical_not(last))
+            def _():
+                wait_far(j)
+
+            @pl.when(last)
+            def _():
+                for i in range(pieces):
+                    for copy in piece_arrivals(i):
+                        copy.wait()
+        else:
+            wait_far(j)
+
+        if j == 1:
+            relay_across()
+        if j == 2:
+            relay_back()
+        for later in STARTS.get(j, ()):
+            start_chunk(later)
+
+        step = min(SIZES[j], 2)
+
+        def heads(turn, carry):
+            for h in range(step):
+                at = (FIRST[j] + turn * step + h) * HD
+                cols = pl.ds(pl.multiple_of(at, HD), HD)
+                query = qbuf[:, :, cols].reshape(2 * tokens, HD)
+                key = kbuf[:, :, cols].reshape(n * tokens, HD)
+                value = vbuf[:, :, cols].reshape(n * tokens, HD)
+                scores = lax.dot_general(
+                    query, key, (((1,), (1,)), ((), ())), preferred_element_type=jnp.float32
+                )
+                highest = jnp.max(scores, axis=1, keepdims=True)
+                weights = jnp.exp2((scores - highest) * factor)
+                totals = jnp.sum(weights, axis=1, keepdims=True)
+                out = jnp.dot(
+                    weights.astype(jnp.bfloat16), value, preferred_element_type=jnp.float32
+                )
+                out = (out / totals).astype(jnp.bfloat16)
+                obuf[:, :, cols] = out.reshape(2, tokens, HD)
+            return carry
+
+        lax.fori_loop(0, SIZES[j] // step, heads, 0)
         for copy in o_copies(j):
             copy.start()
 
-        @pl.when(jnp.logical_and(last, j == LATE))
-        def _():
-            await_rows()
-            lax.fori_loop(0, LATE + 1, project, 0)
-
-        @pl.when(jnp.logical_and(last, j > LATE))
-        def _():
-            project(j, 0)
-
-        return carry
-
-    lax.fori_loop(0, CHUNKS, attend, 0)
+        if j >= LATE:
+            @pl.when(last)
+            def _():
+                if j == LATE:
+                    await_rows()
+                for done in range(0 if j == LATE else j, j + 1):
+                    project(done)
+
+    for j in range(CHUNKS):
+        attend(j)
 
     def noise_copy(c, side):
         return pltpu.make_async_remote_copy(
@@ -373,30 +392,30 @@
                 else:
                     noise_copy(c, side).start()
 
-    def drain(j, carry):
-        cut = jnp.logical_and(last, j == final)
-
-        @pl.when(jnp.logical_not(cut))
-        def _():
-            for dx, dc in far:
-                for copy in kv_copies(dx, dc, j):
-                    copy.wait_send()
-
-        @pl.when(cut)
-        def _():
-            for dx, dc in far:
-                for copy in direct_copies(dx, dc):
-                    copy.wait_send()
-
+    def drain_far(j):
+        for dx, dc in far:
+            for copy in kv_copies(dx, dc, j):
+                copy.wait_send()
+
+    for j in range(CHUNKS):
+        if j == final:
+            @pl.when(jnp.logical_not(last))
+            def _():
+                drain_far(final)
+
+            @pl.when(last)
+            def _():
+                for dx, dc in far:
+                    for copy in direct_copies(dx, dc):
+                        copy.wait_send()
+        else:
+            drain_far(j)
         for copy in kv_copies(0, 1, j):
             copy.wait_send()
         q_copy(j).wait_send()
         local, back = o_copies(j)
         local.wait()
         back.wait()
-        return carry
-
-    lax.fori_loop(0, CHUNKS, drain, 0)
 
     @pl.when(helper)
     def _():
@@ -471,8 +490,8 @@
             pltpu.VMEM((2 * tokens, 1), f32),
             pltpu.VMEM((comps, 2, pad + 8, tokens), f32),
             pltpu.VMEM((2, pad + 8, tokens), f32),
-            pltpu.VMEM((2, 2, tokens // pieces, half // CHUNKS), bf16),
-            pltpu.VMEM((n, 2, tokens // pieces, half // CHUNKS), bf16),
+            pltpu.VMEM((2, 2, tokens // pieces, SIZES[FINAL] * HD), bf16),
+            pltpu.VMEM((n, 2, tokens // pieces, SIZES[FINAL] * HD), bf16),
             pltpu.VMEM((chips, channels, rows_w // w_pieces), bf16),
             dma((n, CHUNKS)), dma((n, CHUNKS)), dma((n, CHUNKS)), dma((n, CHUNKS)),
             dma((CHUNKS,)), dma((CHUNKS,)), dma((CHUNKS,)),

time: 58.3 us -> 59.2 us (1.015)
  Pallas kernels: 55.9 us -> 56.8 us
    pallas_call x1, Pallas kernels: 55.9 us -> 56.8 us  [on_device(): pl.pallas_call(functools.partial(kernel, n, comps, own), out_shape=(pltpu...]
where the time goes in v5:
time: 59.2 us; the launch traced here: 59 us
  Pallas kernels  56.8 us (96%)
  local copies, waits for them, and re-layouts  0.99 us (2%)
  between operations  0.66 us (1%)
  other arithmetic  0.6 us (1%)
    pallas_call x1, Pallas kernels, on_device(): pl.pallas_call(functools.partial(kernel, n, comps, own), out_shape=(pltpu...  56.8 us

profile of v5, /device:TPU:0, one launch (start us, length us, event | category | flops | bytes accessed | tf_op | source)
XLA Modules:
  0.0 59.0 jit_solution(13232126859218418839)
XLA Ops:
  0.6 56.8 %attention_step.1 = (bf16[128,4096]{1,0:T(8,128)(2,1)S(1)}, f32[8,128]{1,0:T(8,128)S(1)}) custom-call(bf16[1,128,4096]{2,1,0:T(8,128)(2,1)} %q_hbm.1, bf16[1,128,4096]{2,1,0:T(8,128)(2,1)} %k_hbm.1, bf16[1,128,4096]{2,1,0:T(8,128)(2,1)} %v_hbm.1, bf16[64,1024]{1,0:T(8,128)(2,1)} %bitcast.3), custom_call_target="tpu_custom_call" | custom-call | tf_op jit(solution)/shard_map/attention_step/pallas_call | solution.py:475
  57.4 0.0 copy-start
  57.5 0.0 copy-start.1
  57.5 1.0 %copy.10 = bf16[1,128,4096]{2,1,0:T(8,128)(2,1)} copy(bf16[1,128,4096]{2,1,0:T(8,128)(2,1)S(1)} %bitcast.2) | data formatting | bytes 2097152
  58.4 0.0 copy-done
  58.4 0.0 copy-done.1
  58.4 0.6 %broadcast_multiply_fusion = (f32[8,128]{1,0:T(8,128)}, f32[8,128]{1,0:T(8,128)}) fusion(f32[8,128]{1,0:T(8,128)S(1)} %copy-done, f32[8,128]{1,0:T(8,128)S(1)} %get-tuple-element.6, f32[8,128]{1,0:T(8,128)S(1)} %copy-done.1), kind=kLoop, calls=%fused_computation.2 | loop fusion | flops 9216 | bytes 20480 | tf_op jit(solution)/shard_map/div | solution.py:510
Async XLA Ops:
  57.4 1.0 %copy-start = (f32[8,128]{1,0:T(8,128)S(1)}, f32[8,128]{1,0:T(8,128)}, u32[]{:S(2)}) copy-start(f32[8,128]{1,0:T(8,128)} %param.9) | copy-start | bytes 12292
  57.5 1.0 %copy-start.1 = (f32[8,128]{1,0:T(8,128)S(1)}, f32[8,128]{1,0:T(8,128)}, u32[]{:S(2)}) copy-start(f32[8,128]{1,0:T(8,128)} %param.10) | copy-start | bytes 12292

commit v6 on v5

--- a/solution.py
+++ b/solution.py
@@ -13,7 +13,7 @@
 CHUNKS = len(SIZES)
 FIRST = tuple(sum(SIZES[:j]) for j in range(CHUNKS))
 FINAL = 3
-LATE = 3
+LATE = 2
 STARTS = {0: (2,), 1: (3,), 2: (4, 5)}
 MESH = pl.DeviceIdType.MESH
 
@@ -322,9 +322,9 @@
         else:
             wait_far(j)
 
+        if j == 0:
+            relay_across()
         if j == 1:
-            relay_across()
-        if j == 2:
             relay_back()
         for later in STARTS.get(j, ()):
             start_chunk(later)
@@ -343,11 +343,11 @@
                 )
                 highest = jnp.max(scores, axis=1, keepdims=True)
                 weights = jnp.exp2((scores - highest) * factor)
-                totals = jnp.sum(weights, axis=1, keepdims=True)
+                wide = jnp.concatenate([value, jnp.ones_like(value)], axis=1)
                 out = jnp.dot(
-                    weights.astype(jnp.bfloat16), value, preferred_element_type=jnp.float32
+                    weights.astype(jnp.bfloat16), wide, preferred_element_type=jnp.float32
                 )
-                out = (out / totals).astype(jnp.bfloat16)
+                out = (out[:, :HD] / out[:, HD:]).astype(jnp.bfloat16)
                 obuf[:, :, cols] = out.reshape(2, tokens, HD)
             return carry
 

time: 59.2 us -> 59.3 us (level)
  no operation moved by 1% of the time
where the time goes in v6:
time: 59.3 us; the launch traced here: 59.2 us
  Pallas kernels  56.9 us (96%)
  local copies, waits for them, and re-layouts  0.99 us (2%)
  between operations  0.66 us (1%)
  other arithmetic  0.6 us (1%)
    pallas_call x1, Pallas kernels, on_device(): pl.pallas_call(functools.partial(kernel, n, comps, own), out_shape=(pltpu...  56.9 us

profile of v6, /device:TPU:0, one launch (start us, length us, event | category | flops | bytes accessed | tf_op | source)
XLA Modules:
  0.0 59.2 jit_solution(14349075257022306314)
XLA Ops:
  0.6 56.9 %attention_step.1 = (bf16[128,4096]{1,0:T(8,128)(2,1)S(1)}, f32[8,128]{1,0:T(8,128)S(1)}) custom-call(bf16[1,128,4096]{2,1,0:T(8,128)(2,1)} %q_hbm.1, bf16[1,128,4096]{2,1,0:T(8,128)(2,1)} %k_hbm.1, bf16[1,128,4096]{2,1,0:T(8,128)(2,1)} %v_hbm.1, bf16[64,1024]{1,0:T(8,128)(2,1)} %bitcast.3), custom_call_target="tpu_custom_call" | custom-call | tf_op jit(solution)/shard_map/attention_step/pallas_call | solution.py:475
  57.6 0.0 copy-start
  57.6 0.0 copy-start.1
  57.6 1.0 %copy.10 = bf16[1,128,4096]{2,1,0:T(8,128)(2,1)} copy(bf16[1,128,4096]{2,1,0:T(8,128)(2,1)S(1)} %bitcast.2) | data formatting | bytes 2097152
  58.6 0.0 copy-done
  58.6 0.0 copy-done.1
  58.6 0.6 %broadcast_multiply_fusion = (f32[8,128]{1,0:T(8,128)}, f32[8,128]{1,0:T(8,128)}) fusion(f32[8,128]{1,0:T(8,128)S(1)} %copy-done, f32[8,128]{1,0:T(8,128)S(1)} %get-tuple-element.6, f32[8,128]{1,0:T(8,128)S(1)} %copy-done.1), kind=kLoop, calls=%fused_computation.2 | loop fusion | flops 9216 | bytes 20480 | tf_op jit(solution)/shard_map/div | solution.py:510
Async XLA Ops:
  57.6 1.0 %copy-start = (f32[8,128]{1,0:T(8,128)S(1)}, f32[8,128]{1,0:T(8,128)}, u32[]{:S(2)}) copy-start(f32[8,128]{1,0:T(8,128)} %param.9) | copy-start | bytes 12292
  57.6 1.0 %copy-start.1 = (f32[8,128]{1,0:T(8,128)S(1)}, f32[8,128]{1,0:T(8,128)}, u32[]{:S(2)}) copy-start(f32[8,128]{1,0:T(8,128)} %param.10) | copy-start | bytes 12292

commit v7 on v4

--- a/solution.py
+++ b/solution.py
@@ -211,6 +211,13 @@
     def start_chunk(j, carry):
         cut = jnp.logical_and(last, j == final)
 
+        def start_mate():
+            for copy in kv_copies(0, 1, j):
+                copy.start()
+            q_copy(j).start()
+
+        pl.when(core == 1)(start_mate)
+
         @pl.when(jnp.logical_not(cut))
         def _():
             for dx, dc in far:
@@ -223,9 +230,7 @@
                 for copy in direct_copies(dx, dc):
                     copy.start()
 
-        for copy in kv_copies(0, 1, j):
-            copy.start()
-        q_copy(j).start()
+        pl.when(core == 0)(start_mate)
         for copy in local_copies(j):
             copy.start()
         return carry

time: 58.3 us -> 58.3 us (level)
  no operation moved by 1% of the time
where the time goes in v7:
time: 58.3 us; the launch traced here: 58.1 us
  Pallas kernels  55.9 us (96%)
  local copies, waits for them, and re-layouts  0.99 us (2%)
  between operations  0.66 us (1%)
  other arithmetic  0.6 us (1%)
    pallas_call x1, Pallas kernels, on_device(): pl.pallas_call(functools.partial(kernel, n, comps, own), out_shape=(pltpu...  55.9 us

profile of v7, /device:TPU:0, one launch (start us, length us, event | category | flops | bytes accessed | tf_op | source)
XLA Modules:
  0.0 58.1 jit_solution(14746848266418627631)
XLA Ops:
  0.6 55.9 %attention_step.1 = (bf16[128,4096]{1,0:T(8,128)(2,1)S(1)}, f32[8,128]{1,0:T(8,128)S(1)}) custom-call(bf16[1,128,4096]{2,1,0:T(8,128)(2,1)} %q_hbm.1, bf16[1,128,4096]{2,1,0:T(8,128)(2,1)} %k_hbm.1, bf16[1,128,4096]{2,1,0:T(8,128)(2,1)} %v_hbm.1, bf16[64,1024]{1,0:T(8,128)(2,1)} %bitcast.3), custom_call_target="tpu_custom_call" | custom-call | tf_op jit(solution)/shard_map/attention_step/pallas_call | solution.py:461
  56.5 0.0 copy-start
  56.5 0.0 copy-start.1
  56.5 1.0 %copy.10 = bf16[1,128,4096]{2,1,0:T(8,128)(2,1)} copy(bf16[1,128,4096]{2,1,0:T(8,128)(2,1)S(1)} %bitcast.2) | data formatting | bytes 2097152
  57.5 0.0 copy-done
  57.5 0.0 copy-done.1
  57.5 0.6 %broadcast_multiply_fusion = (f32[8,128]{1,0:T(8,128)}, f32[8,128]{1,0:T(8,128)}) fusion(f32[8,128]{1,0:T(8,128)S(1)} %copy-done, f32[8,128]{1,0:T(8,128)S(1)} %get-tuple-element.6, f32[8,128]{1,0:T(8,128)S(1)} %copy-done.1), kind=kLoop, calls=%fused_computation.2 | loop fusion | flops 9216 | bytes 20480 | tf_op jit(solution)/shard_map/div | solution.py:496
Async XLA Ops:
  56.5 1.0 %copy-start = (f32[8,128]{1,0:T(8,128)S(1)}, f32[8,128]{1,0:T(8,128)}, u32[]{:S(2)}) copy-start(f32[8,128]{1,0:T(8,128)} %param.9) | copy-start | bytes 12292
  56.5 1.0 %copy-start.1 = (f32[8,128]{1,0:T(8,128)S(1)}, f32[8,128]{1,0:T(8,128)}, u32[]{:S(2)}) copy-start(f32[8,128]{1,0:T(8,128)} %param.10) | copy-start | bytes 12292

commit v8 on v7

--- a/solution.py
+++ b/solution.py
@@ -10,7 +10,7 @@
 
 HD = 128
 CHUNKS = 8
-WINDOW = 2
+WINDOW = 4
 LATE = 5
 MESH = pl.DeviceIdType.MESH
 

time: 58.3 us -> 58.3 us (level)
  no operation moved by 1% of the time
where the time goes in v8:
time: 58.3 us; the launch traced here: 58.1 us
  Pallas kernels  55.9 us (96%)
  local copies, waits for them, and re-layouts  0.99 us (2%)
  between operations  0.66 us (1%)
  other arithmetic  0.6 us (1%)
    pallas_call x1, Pallas kernels, on_device(): pl.pallas_call(functools.partial(kernel, n, comps, own), out_shape=(pltpu...  55.9 us

profile of v8, /device:TPU:0, one launch (start us, length us, event | category | flops | bytes accessed | tf_op | source)
XLA Modules:
  0.0 58.1 jit_solution(9818658486081048468)
XLA Ops:
  0.6 55.9 %attention_step.1 = (bf16[128,4096]{1,0:T(8,128)(2,1)S(1)}, f32[8,128]{1,0:T(8,128)S(1)}) custom-call(bf16[1,128,4096]{2,1,0:T(8,128)(2,1)} %q_hbm.1, bf16[1,128,4096]{2,1,0:T(8,128)(2,1)} %k_hbm.1, bf16[1,128,4096]{2,1,0:T(8,128)(2,1)} %v_hbm.1, bf16[64,1024]{1,0:T(8,128)(2,1)} %bitcast.3), custom_call_target="tpu_custom_call" | custom-call | tf_op jit(solution)/shard_map/attention_step/pallas_call | solution.py:461
  56.5 0.0 copy-start
  56.5 0.0 copy-start.1
  56.5 1.0 %copy.10 = bf16[1,128,4096]{2,1,0:T(8,128)(2,1)} copy(bf16[1,128,4096]{2,1,0:T(8,128)(2,1)S(1)} %bitcast.2) | data formatting | bytes 2097152
  57.5 0.0 copy-done
  57.5 0.0 copy-done.1
  57.5 0.6 %broadcast_multiply_fusion = (f32[8,128]{1,0:T(8,128)}, f32[8,128]{1,0:T(8,128)}) fusion(f32[8,128]{1,0:T(8,128)S(1)} %copy-done, f32[8,128]{1,0:T(8,128)S(1)} %get-tuple-element.6, f32[8,128]{1,0:T(8,128)S(1)} %copy-done.1), kind=kLoop, calls=%fused_computation.2 | loop fusion | flops 9216 | bytes 20480 | tf_op jit(solution)/shard_map/div | solution.py:496
Async XLA Ops:
  56.5 1.0 %copy-start = (f32[8,128]{1,0:T(8,128)S(1)}, f32[8,128]{1,0:T(8,128)}, u32[]{:S(2)}) copy-start(f32[8,128]{1,0:T(8,128)} %param.9) | copy-start | bytes 12292
  56.5 1.0 %copy-start.1 = (f32[8,128]{1,0:T(8,128)S(1)}, f32[8,128]{1,0:T(8,128)}, u32[]{:S(2)}) copy-start(f32[8,128]{1,0:T(8,128)} %param.10) | copy-start | bytes 12292
